TPU v7x, 512 devices: a whole 4x8x8 slice. The times are simulated.
512 devices in a mesh: rep: 16 (over x, z_hi), feat: 32 (over z_lo, y, core).
Axes of the slice: x: 4, y: 8, z: 8 (z_hi: 4, z_lo: 2; z = z_hi * 2 + z_lo), core: 2. Of those that a mesh axis runs over, the one named last changes fastest.
Arguments:
- basis: float32 [16, 64, 131072], P('rep', None, 'feat'), may hold values from -6 to 6
- stream: bfloat16 [16, 2, 128, 131072], P('rep', None, None, 'feat'), may hold values from -6 to 6
Outputs:
- new_basis: float32 [16, 64, 131072], P('rep', None, 'feat')
All inputs are finite; a program needn't handle non-finite values.
Results may differ from a plain program's by a relative error of at most 0.0003.
Values sent between devices are 32-bit elements; how exact they have to be, the bound alone decides.
No kernel may reach another device: no remote copies, remote signals or barrier semaphores. Data moves between devices by JAX's collectives and lax.ppermute only.
A program may use at most 64 MiB of HBM per device.

v0:
```python
import jax
import jax.numpy as jnp
from jax import lax
from jax.sharding import PartitionSpec as P

FEAT_DEV = 4096
learn_rate = 0.5


def high_dot(left, right):
    return jnp.dot(left, right, precision=lax.Precision.HIGHEST, preferred_element_type=jnp.float32)


def step_sum(partial_value):
    return lax.psum(partial_value, "feat")


def advance(current, proj, rows, step_size):
    cov = high_dot(proj.T, proj)
    drive = high_dot(proj.T, rows)
    shrink = high_dot(cov, current)
    return current + step_size * (drive - shrink)


def per_device(basis, stream):
    start = basis[0]
    batches = stream[0]
    steps_here = batches.shape[0]
    batch_rows = batches.shape[1]
    total_feat = FEAT_DEV * lax.axis_size("feat")
    scale = jnp.sqrt(jnp.float32(total_feat))
    step_size = learn_rate / batch_rows
    current = start
    for step in range(steps_here):
        rows = batches[step]
        proj = step_sum(high_dot(rows, current.T)) / scale
        current = advance(current, proj, rows, step_size)
    replicas = lax.axis_size("rep")
    average = lax.psum(basis, "rep")[0] / replicas
    mixed = current + average - start
    gram = lax.psum(high_dot(mixed, mixed.T), "feat") / total_feat
    lower = jnp.linalg.cholesky(gram)
    result = lax.linalg.triangular_solve(lower, mixed, left_side=True, lower=True)
    return result[None]


def solution(mesh):
    placed = (P("rep", None, "feat"), P("rep", None, None, "feat"))
    return jax.shard_map(
        per_device, mesh=mesh, in_specs=placed, out_specs=P("rep", None, "feat"), check_vma=False
    )
```

profile of v0, /device:TPU:1, one launch (start us, length us, event | category | flops | bytes accessed | tf_op | source)
XLA Modules:
  0.0 365.0 jit_solution(18399803514366530212)
XLA Ops:
  6.5 0.0 all-reduce.2.cloned.1.call-start
  6.5 0.7 all-reduce.2.cloned.1.call-update
  7.3 0.0 copy-start
  7.3 2.8 fusion.11
  10.1 109.9 %psum.28 = f32[128,64]{0,1:T(8,128)S(1)} all-reduce(f32[128,64]{0,1:T(8,128)S(1)} %fusion.11), channel_id=1, replica_groups=mesh['rep'=16,'feat'=32] {'feat'}, use_global_device_ids=true, to_apply=%region_0.0 | all-reduce | flops 8192 | bytes 65536 | tf_op jit(solution)/shard_map/psum | solution.py:15
  120.0 0.2 fusion.25
  120.2 1.8 fusion.9
  122.0 0.0 copy-done
  122.0 0.0 copy-start.1
  122.0 1.1 fusion.3
  123.1 0.5 copy-done.1
  123.6 1.2 convolution_bitcast_fusion.1
  124.8 108.1 %psum.29 = f32[128,64]{0,1:T(8,128)S(1)} all-reduce(f32[128,64]{0,1:T(8,128)S(1)} %convolution_bitcast_fusion.1), channel_id=1, replica_groups=mesh['rep'=16,'feat'=32] {'feat'}, use_global_device_ids=true, to_apply=%region_1.0 | all-reduce | flops 8192 | bytes 65536 | tf_op jit(solution)/shard_map/psum | solution.py:15
  232.9 0.2 fusion.22
  233.1 2.8 fusion.6
  235.8 2.7 fusion.5
  238.6 1.0 fusion.36
  239.6 104.4 %psum.31 = f32[64,64]{0,1:T(8,128)S(1)} all-reduce(f32[64,64]{0,1:T(8,128)S(1)} %fusion.36), channel_id=1, replica_groups=mesh['rep'=16,'feat'=32] {'feat'}, use_global_device_ids=true, to_apply=%region_3.0 | all-reduce | flops 4096 | bytes 32768 | tf_op jit(solution)/shard_map/psum | solution.py:41
  344.0 0.1 copy.4
  344.1 5.8 %cholesky.16 = f32[64,64]{1,0:T(8,128)S(1)} custom-call(f32[64,64]{1,0:T(8,128)S(1)} %fusion.21), custom_call_target="Cholesky" | custom-call | tf_op jit(solution)/shard_map/jit(cholesky)/cholesky | solution.py:42
  350.0 0.6 compare_reduce_fusion
  350.6 0.7 fusion.19
  351.3 4.9 %custom-call.6 = f32[1,64,64]{1,2,0:T(8,128)S(1)} custom-call(f32[1,64,64]{2,1,0:T(8,128)S(1)} %fusion.19), custom_call_target="InvertDiagBlocksLowerTriangular" | custom-call | tf_op jit(solution)/shard_map/triangular_solve | solution.py:43
  356.2 2.0 convolution_bitcast_fusion
  (4 shorter events, 0.0 us)
Async XLA Ops:
  6.5 229.3 %all-reduce.2.cloned.1.call-start = ((), (), s32[]{:S(2)}) async-start(), calls=%async_computation | async-start | bytes 2097152 | tf_op jit(solution)/shard_map/psum | solution.py:39
  7.3 114.8 %copy-start = (f32[1,64,4096]{2,1,0:T(8,128)S(1)}, f32[1,64,4096]{2,1,0:T(8,128)}, u32[]{:S(2)}) copy-start(f32[1,64,4096]{2,1,0:T(8,128)} %param.2) | copy-start | bytes 3145732
  122.0 1.6 copy-start.1
Sparse Core Ops, SparseCore 0:
  10.3 171.0 all-reduce.1
where the time goes:
time: 365 us
  blocking collectives  322 us (88%)
  matrix products  15.7 us (4%)
  between operations  13.5 us (4%)
  other arithmetic  12.1 us (3%)
    psum x2, blocking collectives, step_sum(): return lax.psum(partial_value, 'feat')  218 us
    psum x1, blocking collectives, per_device(): gram = lax.psum(high_dot(mixed, mixed.T), 'feat') / total_feat  104 us
    dot_general x9, matrix products, high_dot(): jnp.dot(left, right, precision=lax.Precision.HIGHEST, preferred_element_t...  13.7 us
  transfers between devices with their start and end apart: 1, of which 0 were waited for; matrix products, arithmetic and copies ran while one was open for 3% of the time, Pallas kernels for 0%

commit v1 on v0

--- a/solution.py
+++ b/solution.py
@@ -38,7 +38,7 @@
     replicas = lax.axis_size("rep")
     average = lax.psum(basis, "rep")[0] / replicas
     mixed = current + average - start
-    gram = lax.psum(high_dot(mixed, mixed.T), "feat") / total_feat
+    gram = jnp.sum(lax.all_gather(high_dot(mixed, mixed.T), "feat"), axis=0) / total_feat
     lower = jnp.linalg.cholesky(gram)
     result = lax.linalg.triangular_solve(lower, mixed, left_side=True, lower=True)
     return result[None]

time: 365 us -> 299 us (0.82)
  blocking collectives: 322 us -> 256 us
    psum x1 -> x0, blocking collectives: 104 us -> none  [per_device(): gram = lax.psum(high_dot(mixed, mixed.T), 'feat') / total_feat]
    all_gather x0 -> x1, blocking collectives: none -> 37.7 us  [per_device(): lax.all_gather(high_dot(mixed, mixed.T), 'feat')]
where the time goes in v1:
time: 299 us; the launch traced here: 298 us
  blocking collectives  256 us (86%)
  matrix products  15.7 us (5%)
  between operations  13.5 us (5%)
  other arithmetic  12.2 us (4%)
    psum x2, blocking collectives, step_sum(): return lax.psum(partial_value, 'feat')  218 us
    all_gather x1, blocking collectives, per_device(): lax.all_gather(high_dot(mixed, mixed.T), 'feat')  37.7 us
    dot_general x9, matrix products, high_dot(): jnp.dot(left, right, precision=lax.Precision.HIGHEST, preferred_element_t...  13.7 us
    another operation x3, other arithmetic, per_device(): lower = jnp.linalg.cholesky(gram)  6.52 us
  transfers between devices with their start and end apart: 1, of which 0 were waited for; matrix products, arithmetic and copies ran while one was open for 3% of the time, Pallas kernels for 0%

profile of v1, /device:TPU:1, one launch (start us, length us, event | category | flops | bytes accessed | tf_op | source)
XLA Modules:
  0.0 298.4 jit_solution(3826956122840111161)
XLA Ops:
  6.5 0.0 all-reduce.2.cloned.1.call-start
  6.5 0.7 all-reduce.2.cloned.1.call-update
  7.3 2.8 fusion.11
  10.1 109.9 %psum.21 = f32[128,64]{0,1:T(8,128)S(1)} all-reduce(f32[128,64]{0,1:T(8,128)S(1)} %fusion.11), channel_id=1, replica_groups=mesh['rep'=16,'feat'=32] {'feat'}, use_global_device_ids=true, to_apply=%region_0.0 | all-reduce | flops 8192 | bytes 65536 | tf_op jit(solution)/shard_map/psum | solution.py:15
  120.0 0.2 fusion.25
  120.2 1.8 fusion.9
  122.0 0.0 copy-done
  122.0 0.0 copy-start.1
  122.0 1.1 fusion.3
  123.1 0.5 copy-done.1
  123.6 1.2 convolution_bitcast_fusion.1
  124.8 108.1 %psum.22 = f32[128,64]{0,1:T(8,128)S(1)} all-reduce(f32[128,64]{0,1:T(8,128)S(1)} %convolution_bitcast_fusion.1), channel_id=1, replica_groups=mesh['rep'=16,'feat'=32] {'feat'}, use_global_device_ids=true, to_apply=%region_1.0 | all-reduce | flops 8192 | bytes 65536 | tf_op jit(solution)/shard_map/psum | solution.py:15
  232.9 0.2 fusion.22
  233.1 2.8 fusion.6
  235.8 2.7 fusion.5
  238.6 1.0 fusion.36
  239.6 37.7 %all-gather = f32[2048,64]{1,0:T(8,128)S(1)} all-gather(f32[64,64]{1,0:T(8,128)S(1)} %fusion.36), channel_id=2, replica_groups=mesh['rep'=16,'feat'=32] {'feat'}, dimensions={0}, use_global_device_ids=true | all-gather | bytes 540672 | tf_op jit(solution)/shard_map/all_gather | solution.py:41
  277.2 0.1 reduce_sum.11
  277.3 0.1 copy.4
  277.4 5.8 %cholesky.16 = f32[64,64]{1,0:T(8,128)S(1)} custom-call(f32[64,64]{1,0:T(8,128)S(1)} %fusion.21), custom_call_target="Cholesky" | custom-call | tf_op jit(solution)/shard_map/jit(cholesky)/cholesky | solution.py:42
  283.3 0.6 compare_reduce_fusion
  283.9 0.7 fusion.19
  284.6 4.9 %custom-call.6 = f32[1,64,64]{1,2,0:T(8,128)S(1)} custom-call(f32[1,64,64]{2,1,0:T(8,128)S(1)} %fusion.19), custom_call_target="InvertDiagBlocksLowerTriangular" | custom-call | tf_op jit(solution)/shard_map/triangular_solve | solution.py:43
  289.5 2.0 convolution_bitcast_fusion
  (4 shorter events, 0.0 us)
Async XLA Ops:
  6.5 229.3 %all-reduce.2.cloned.1.call-start = ((), (), s32[]{:S(2)}) async-start(), calls=%async_computation | async-start | bytes 2097152 | tf_op jit(solution)/shard_map/psum | solution.py:39
  7.3 114.8 %copy-start = (f32[1,64,4096]{2,1,0:T(8,128)S(1)}, f32[1,64,4096]{2,1,0:T(8,128)}, u32[]{:S(2)}) copy-start(f32[1,64,4096]{2,1,0:T(8,128)} %param.2) | copy-start | bytes 3145732
  122.0 1.6 copy-start.1
Sparse Core Ops, SparseCore 0:
  10.3 171.0 all-reduce.1
